TPU v7x, 512 devices: a whole 4x4x16 slice. The times are simulated.
512 devices in a mesh: row: 64 (over z_hi, y, x, core), col: 8 (over z_lo).
Axes of the slice: x: 4, y: 4, z: 16 (z_hi: 2, z_lo: 8; z = z_hi * 8 + z_lo), core: 2. Of those that a mesh axis runs over, the one named last changes fastest.
Arguments:
- air_state: bfloat16 [65536, 384], P(('row', 'col')), may hold values from -6 to 6
- owner_map: int32 [65536, 1], P(('row', 'col')), may hold values from 0 to 63; in each aligned block of 128 rows (0 to 127, 128 to 255, ...) at most 4 rows name the same one
- cost_class: int32 [65536], P(('row', 'col')), may hold values from 0 to 3
- connectivity: int32 [4, 65536], P(None, ('row', 'col')), may hold values from -32 to 32, as said below
- inverse_blocks: bfloat16 [512, 4, 3, 128, 128], P(('row', 'col')), may hold values from -0.5 to 0.5
Outputs:
- new_state: bfloat16 [65536, 384], P(('row', 'col'))
Inputs may be any that keep to these rules, and one draw needn't show every extreme that they name: `owner_map`: among the columns of one device no owner row is named by more than 4 columns, and some owner row is named by exactly 4. `connectivity`: offsets are never zero; both ends of the range occur.
All inputs are finite; a program needn't handle non-finite values.
Results may differ from a plain program's by a relative error of at most 0.0037.
Values may be sent and summed in bfloat16 or wider, within the bound.
A program may use at most 128 MiB of HBM per device.

v0:
```python
import math

import jax
import jax.numpy as jnp
from jax import lax
from jax.sharding import PartitionSpec as P

viscosity = 0.25


def padded(cells, sides, width):
    for axis, dim in sides:
        count = lax.axis_size(axis)
        head = lax.slice_in_dim(cells, 0, width, axis=dim)
        tail = lax.slice_in_dim(cells, cells.shape[dim] - width, cells.shape[dim], axis=dim)
        cells = jnp.concatenate(
            [
                lax.ppermute(tail, axis, [(i, (i + 1) % count) for i in range(count)]),
                cells,
                lax.ppermute(head, axis, [((i + 1) % count, i) for i in range(count)]),
            ],
            axis=dim,
        )
    return cells


def apply_local(received, labels_in, inverse_blocks):
    layout_shape = received.shape
    levels = inverse_blocks.shape[-1]
    classes = inverse_blocks.shape[1]
    slot_total = layout_shape[0] * layout_shape[1]
    fields = received.reshape(slot_total, 3, levels)
    labels = labels_in.reshape(slot_total)
    block_rows = math.gcd(256, slot_total)
    class_values = jnp.arange(classes, dtype=jnp.int32).astype(jnp.bfloat16)
    own_blocks = inverse_blocks[0]

    def one_block(pair):
        field_block, label_block = pair
        selector = (label_block[:, None] == class_values[None, :]).astype(jnp.bfloat16)
        spread = field_block[:, None, :, :] * selector[:, :, None, None]
        result = jnp.einsum(
            "rcfm,cflm->rfl", spread, own_blocks, preferred_element_type=jnp.float32
        )
        return result.astype(jnp.bfloat16)

    computed = lax.map(
        one_block, (fields.reshape(-1, block_rows, 3, levels), labels.reshape(-1, block_rows))
    )
    return computed.reshape(layout_shape)


def pack_slots(air_state, targets, slot_index, cost_class, groups, capacity):
    outgoing = (
        jnp.zeros((groups, capacity, air_state.shape[1]), jnp.bfloat16)
        .at[targets, slot_index]
        .set(air_state)
    )
    labels_out = (
        jnp.full((groups, capacity), -1.0, jnp.bfloat16)
        .at[targets, slot_index]
        .set(cost_class.astype(jnp.bfloat16))
    )
    return (outgoing, labels_out)


def per_device(air_state, owner_map, cost_class, connectivity, inverse_blocks):
    groups = lax.axis_size("row")
    local_count = air_state.shape[0]
    capacity = 2 * local_count // groups
    targets = owner_map[:, 0]
    target_hits = (targets[:, None] == jnp.arange(groups, dtype=jnp.int32)[None, :]).astype(
        jnp.int32
    )
    slot_index = jnp.sum((jnp.cumsum(target_hits, axis=0) - 1) * target_hits, axis=1)
    halo_width = local_count // 4
    extended = padded(air_state, (("col", 0),), halo_width)
    center = air_state.astype(jnp.float32)
    places = jnp.arange(local_count, dtype=jnp.int32) + halo_width
    laplace_sum = jnp.zeros_like(center)
    for partner in range(connectivity.shape[0]):
        laplace_sum = laplace_sum + (
            extended[places + connectivity[partner]].astype(jnp.float32) - center
        )
    outgoing, labels_out = pack_slots(air_state, targets, slot_index, cost_class, groups, capacity)
    received, labels_in = (
        lax.all_to_all(outgoing, "row", split_axis=0, concat_axis=0, tiled=True),
        lax.all_to_all(labels_out, "row", split_axis=0, concat_axis=0, tiled=True),
    )
    computed = apply_local(received, labels_in, inverse_blocks)
    returned = lax.all_to_all(computed, "row", split_axis=0, concat_axis=0, tiled=True)
    physics = returned[targets, slot_index]
    return (physics.astype(jnp.float32) + viscosity * laplace_sum).astype(jnp.bfloat16)


def solution(mesh):
    return jax.shard_map(
        per_device,
        mesh=mesh,
        in_specs=(
            P(("row", "col"), None),
            P(("row", "col"), None),
            P(("row", "col")),
            P(None, ("row", "col")),
            P(("row", "col"), None, None, None, None),
        ),
        out_specs=P(("row", "col"), None),
        check_vma=False,
    )
```

profile of v0, /device:TPU:33, one launch (start us, length us, event | category | flops | bytes accessed | tf_op | source)
XLA Modules:
  0.0 117.7 jit_solution(6084306007919625231)
XLA Ops:
  0.0 0.7 copy-done.2
  0.8 0.2 reduce_window_sum.11
  1.2 0.6 copy-done.4
  1.8 6.6 %scatter_fusion.1 = bf16[64,4]{0,1:T(4,128)(2,1)S(1)} fusion(bf16[64,4]{0,1:T(4,128)(2,1)S(1)} %broadcast_in_dim.11, s32[128]{0:T(128)S(1)} %get-tuple-element.15, bf16[128]{0:T(256)(128)(2,1)S(1)} %convert_element_type.50), kind=kCustom, calls=%fused_computation.6 | custom fusion | bytes 1792 | tf_op jit(solution)/shard_map/scatter | solution.py:62
  8.4 0.7 copy.12
  9.2 20.5 %all-to-all-start.1 = ((bf16[64,1,4]{2,1,0:T(2,128)(2,1)}), bf16[64,1,4]{2,1,0:T(2,128)(2,1)S(1)}, u32[]{:S(2)}, u32[]{:S(2)}) async-start(bf16[64,1,4]{2,1,0:T(2,128)(2,1)} %copy.12), calls=%async_computation.1 | async-start | bytes 65536 | tf_op jit(solution)/shard_map/all_to_all | solution.py:88
  29.7 0.7 broadcast_in_dim.10
  30.6 15.2 %scatter_fusion = bf16[64,4,384]{2,1,0:T(4,128)(2,1)} fusion(bf16[64,4,384]{2,1,0:T(4,128)(2,1)} %broadcast_in_dim.10, s32[128]{0:T(128)S(1)} %get-tuple-element.15, bf16[128,384]{1,0:T(8,128)(2,1)S(1)} %copy-done.1), kind=kCustom, calls=%fused_computation.5 | custom fusion | bytes 295936 | tf_op jit(solution)/shard_map/scatter | solution.py:57
  45.8 0.4 all-to-all-done.1
  46.2 17.3 %all-to-all-start = ((bf16[64,4,384]{2,1,0:T(4,128)(2,1)}), bf16[64,4,384]{2,1,0:T(4,128)(2,1)S(1)}, u32[]{:S(2)}, u32[]{:S(2)}) async-start(bf16[64,4,384]{2,1,0:T(4,128)(2,1)} %scatter_fusion), calls=%async_computation | async-start | bytes 393216 | tf_op jit(solution)/shard_map/all_to_all | solution.py:87
  63.5 2.7 %collective-permute-start = (bf16[32,384]{1,0:T(8,128)(2,1)S(1)}, bf16[32,384]{1,0:T(8,128)(2,1)S(1)}, u32[]{:S(2)}, u32[]{:S(2)}) collective-permute-start(bf16[32,384]{1,0:T(8,128)(2,1)S(1)} %get-tuple-element.24), channel_id=1, source_target_pairs={{0,1},{1,2},{2,3},{3,4},{4,5},{5,6},{6,7},{7,0},{8,9},{9,10},{10,1... | collective-permute-start | bytes 73736 | tf_op jit(solution)/shard_map/ppermute | solution.py:18
  66.1 2.6 %collective-permute-start.1 = (bf16[32,384]{1,0:T(8,128)(2,1)S(1)}, bf16[32,384]{1,0:T(8,128)(2,1)S(1)}, u32[]{:S(2)}, u32[]{:S(2)}) collective-permute-start(bf16[32,384]{1,0:T(8,128)(2,1)S(1)} %get-tuple-element.17), channel_id=1, source_target_pairs={{1,0},{2,1},{3,2},{4,3},{5,4},{6,5},{7,6},{0,7},{9,8},{10,9},{11,1... | collective-permute-start | bytes 73736 | tf_op jit(solution)/shard_map/ppermute | solution.py:20
  69.1 18.6 %all-to-all-done = bf16[64,4,384]{2,1,0:T(4,128)(2,1)S(1)} async-done(((bf16[64,4,384]{2,1,0:T(4,128)(2,1)}), bf16[64,4,384]{2,1,0:T(4,128)(2,1)S(1)}, u32[]{:S(2)}, u32[]{:S(2)}) %all-to-all-start) | async-done | bytes 196640 | tf_op jit(solution)/shard_map/all_to_all | solution.py:87
  87.8 0.5 fusion.1
  88.3 0.2 copy.14
  88.4 0.8 reshape.147
  89.3 4.6 %all-to-all-start.2 = ((bf16[64,4,384]{2,1,0:T(4,128)(2,1)}), bf16[64,4,384]{2,1,0:T(4,128)(2,1)S(1)}, u32[]{:S(2)}, u32[]{:S(2)}) async-start(bf16[64,4,384]{2,1,0:T(4,128)(2,1)} %reshape.147), calls=%async_computation.2 | async-start | bytes 393216 | tf_op jit(solution)/shard_map/all_to_all | solution.py:91
  94.0 0.9 gather_fusion.1
  94.9 0.9 gather_fusion.2
  95.7 0.9 gather_fusion.3
  96.6 0.9 gather_fusion.4
  97.5 18.2 %all-to-all-done.2 = bf16[64,4,384]{2,1,0:T(4,128)(2,1)S(1)} async-done(((bf16[64,4,384]{2,1,0:T(4,128)(2,1)}), bf16[64,4,384]{2,1,0:T(4,128)(2,1)S(1)}, u32[]{:S(2)}, u32[]{:S(2)}) %all-to-all-start.2) | async-done | bytes 196640 | tf_op jit(solution)/shard_map/all_to_all | solution.py:91
  115.7 1.2 %gather_fusion = bf16[128,384]{1,0:T(8,128)(2,1)S(1)} fusion(bf16[64,4,384]{2,1,0:T(4,128)(2,1)S(1)} %all-to-all-done.2, s32[128]{0:T(128)S(1)} %bitcast.50), kind=kCustom, calls=%fused_computation | custom fusion | bytes 197632 | tf_op jit(solution)/shard_map/gather | solution.py:92
  116.9 0.7 fusion.11
  (28 shorter events, 0.9 us)
Async XLA Ops:
  0.0 87.8 %copy-start = (bf16[1,4,3,128,128]{4,3,2,1,0:T(8,128)(2,1)S(1)}, bf16[1,4,3,128,128]{4,3,2,1,0:T(8,128)(2,1)}, u32[]{:S(2)}) copy-start(bf16[1,4,3,128,128]{4,3,2,1,0:T(8,128)(2,1)} %param.9) | copy-start | bytes 1179652
  0.0 0.7 copy-start.2
  1.1 0.7 copy-start.4
  9.2 37.0 %all-to-all-start.1 = ((bf16[64,1,4]{2,1,0:T(2,128)(2,1)}), bf16[64,1,4]{2,1,0:T(2,128)(2,1)S(1)}, u32[]{:S(2)}, u32[]{:S(2)}) async-start(bf16[64,1,4]{2,1,0:T(2,128)(2,1)} %copy.12), calls=%async_computation.1 | async-start | bytes 65536 | tf_op jit(solution)/shard_map/all_to_all | solution.py:88
  29.7 0.9 copy-start.1
  46.2 41.5 %all-to-all-start = ((bf16[64,4,384]{2,1,0:T(4,128)(2,1)}), bf16[64,4,384]{2,1,0:T(4,128)(2,1)S(1)}, u32[]{:S(2)}, u32[]{:S(2)}) async-start(bf16[64,4,384]{2,1,0:T(4,128)(2,1)} %scatter_fusion), calls=%async_computation | async-start | bytes 393216 | tf_op jit(solution)/shard_map/all_to_all | solution.py:87
  63.5 30.5 %collective-permute-start = (bf16[32,384]{1,0:T(8,128)(2,1)S(1)}, bf16[32,384]{1,0:T(8,128)(2,1)S(1)}, u32[]{:S(2)}, u32[]{:S(2)}) collective-permute-start(bf16[32,384]{1,0:T(8,128)(2,1)S(1)} %get-tuple-element.24), channel_id=1, source_target_pairs={{0,1},{1,2},{2,3},{3,4},{4,5},{5,6},{6,7},{7,0},{8,9},{9,10},{10,1... | collective-permute-start | bytes 73736 | tf_op jit(solution)/shard_map/ppermute | solution.py:18
  66.1 27.8 %collective-permute-start.1 = (bf16[32,384]{1,0:T(8,128)(2,1)S(1)}, bf16[32,384]{1,0:T(8,128)(2,1)S(1)}, u32[]{:S(2)}, u32[]{:S(2)}) collective-permute-start(bf16[32,384]{1,0:T(8,128)(2,1)S(1)} %get-tuple-element.17), channel_id=1, source_target_pairs={{1,0},{2,1},{3,2},{4,3},{5,4},{6,5},{7,6},{0,7},{9,8},{10,9},{11,1... | collective-permute-start | bytes 73736 | tf_op jit(solution)/shard_map/ppermute | solution.py:20
  89.3 4.6 %copy-start.3 = (s32[4,128]{1,0:T(4,128)S(1)}, s32[4,128]{1,0:T(4,128)}, u32[]{:S(2)}) copy-start(s32[4,128]{1,0:T(4,128)} %param.8) | copy-start | bytes 6148
  89.3 26.4 %all-to-all-start.2 = ((bf16[64,4,384]{2,1,0:T(4,128)(2,1)}), bf16[64,4,384]{2,1,0:T(4,128)(2,1)S(1)}, u32[]{:S(2)}, u32[]{:S(2)}) async-start(bf16[64,4,384]{2,1,0:T(4,128)(2,1)} %reshape.147), calls=%async_computation.2 | async-start | bytes 393216 | tf_op jit(solution)/shard_map/all_to_all | solution.py:91
where the time goes:
time: 118 us
  starting transfers between devices  47.6 us (40%)
  waiting for transfers between devices  37.2 us (32%)
  local copies, waits for them, and re-layouts  30.8 us (26%)
  other arithmetic  1.39 us (1%)
    all_to_all x1, starting transfers between devices, per_device(): lax.all_to_all(labels_out, 'row', split_axis=0, concat_axis=0, tiled=True)  20.5 us
    all_to_all x1, waiting for transfers between devices, per_device(): lax.all_to_all(outgoing, 'row', split_axis=0, concat_axis=0, tiled=True)  18.6 us
    all_to_all x1, waiting for transfers between devices, per_device(): lax.all_to_all(computed, 'row', split_axis=0, concat_axis=0, tiled=True)  18.2 us
    all_to_all x1, starting transfers between devices, per_device(): lax.all_to_all(outgoing, 'row', split_axis=0, concat_axis=0, tiled=True)  17.3 us
    scatter x1, local copies, waits for them, and re-layouts, pack_slots(): outgoing = jnp.zeros((groups, capacity, air_state.shape[1]), jnp.bfloat16...  15.2 us
    scatter x1, local copies, waits for them, and re-layouts, pack_slots(): labels_out = jnp.full((groups, capacity), -1.0, jnp.bfloat16).at[targets,...  6.61 us
    all_to_all x1, starting transfers between devices, per_device(): lax.all_to_all(computed, 'row', split_axis=0, concat_axis=0, tiled=True)  4.58 us
    gather x4, local copies, waits for them, and re-layouts, per_device(): extended[places + connectivity[partner]].astype(jnp.float32) - center  3.46 us
  transfers between devices with their start and end apart: 5, of which 3 were waited for; matrix products, arithmetic and copies ran while one was open for 18% of the time, Pallas kernels for 0%

commit v1 on v0

--- a/solution.py
+++ b/solution.py
@@ -69,10 +69,9 @@
     local_count = air_state.shape[0]
     capacity = 2 * local_count // groups
     targets = owner_map[:, 0]
-    target_hits = (targets[:, None] == jnp.arange(groups, dtype=jnp.int32)[None, :]).astype(
-        jnp.int32
-    )
-    slot_index = jnp.sum((jnp.cumsum(target_hits, axis=0) - 1) * target_hits, axis=1)
+    earlier = jnp.arange(local_count)[:, None] > jnp.arange(local_count)[None, :]
+    same = targets[:, None] == targets[None, :]
+    slot_index = jnp.sum((earlier & same).astype(jnp.int32), axis=1)
     halo_width = local_count // 4
     extended = padded(air_state, (("col", 0),), halo_width)
     center = air_state.astype(jnp.float32)

time: 118 us -> 118 us (level)
  no operation moved by 1% of the time
where the time goes in v1:
time: 118 us; the launch traced here: 117 us
  starting transfers between devices  47.6 us (40%)
  waiting for transfers between devices  37.1 us (31%)
  local copies, waits for them, and re-layouts  30.9 us (26%)
    all_to_all x1, starting transfers between devices, per_device(): lax.all_to_all(labels_out, 'row', split_axis=0, concat_axis=0, tiled=True)  20.5 us
    all_to_all x1, waiting for transfers between devices, per_device(): lax.all_to_all(outgoing, 'row', split_axis=0, concat_axis=0, tiled=True)  18.6 us
    all_to_all x1, waiting for transfers between devices, per_device(): lax.all_to_all(computed, 'row', split_axis=0, concat_axis=0, tiled=True)  18.2 us
    all_to_all x1, starting transfers between devices, per_device(): lax.all_to_all(outgoing, 'row', split_axis=0, concat_axis=0, tiled=True)  17.3 us
    scatter x1, local copies, waits for them, and re-layouts, pack_slots(): outgoing = jnp.zeros((groups, capacity, air_state.shape[1]), jnp.bfloat16...  15.3 us
    scatter x1, local copies, waits for them, and re-layouts, pack_slots(): labels_out = jnp.full((groups, capacity), -1.0, jnp.bfloat16).at[targets,...  6.61 us
    all_to_all x1, starting transfers between devices, per_device(): lax.all_to_all(computed, 'row', split_axis=0, concat_axis=0, tiled=True)  4.58 us
    gather x4, local copies, waits for them, and re-layouts, per_device(): extended[places + connectivity[partner]].astype(jnp.float32) - center  3.46 us
  transfers between devices with their start and end apart: 5, of which 3 were waited for; matrix products, arithmetic and copies ran while one was open for 18% of the time, Pallas kernels for 0%

profile of v1, /device:TPU:33, one launch (start us, length us, event | category | flops | bytes accessed | tf_op | source)
XLA Modules:
  0.0 117.4 jit_solution(17893444048399850250)
XLA Ops:
  0.0 0.7 copy-done.3
  0.7 0.2 convert_reduce_fusion
  0.9 0.6 copy-done.4
  1.6 6.6 %scatter_fusion.1 = bf16[64,4]{0,1:T(4,128)(2,1)S(1)} fusion(bf16[64,4]{0,1:T(4,128)(2,1)S(1)} %broadcast_in_dim.11, s32[128]{0:T(128)S(1)} %get-tuple-element.15, bf16[128]{0:T(256)(128)(2,1)S(1)} %convert_element_type.50), kind=kCustom, calls=%fused_computation.6 | custom fusion | bytes 1792 | tf_op jit(solution)/shard_map/scatter | solution.py:62
  8.2 0.7 copy.16
  8.9 20.5 %all-to-all-start.1 = ((bf16[64,1,4]{2,1,0:T(2,128)(2,1)}), bf16[64,1,4]{2,1,0:T(2,128)(2,1)S(1)}, u32[]{:S(2)}, u32[]{:S(2)}) async-start(bf16[64,1,4]{2,1,0:T(2,128)(2,1)} %copy.16), calls=%async_computation.1 | async-start | bytes 65536 | tf_op jit(solution)/shard_map/all_to_all | solution.py:87
  29.4 0.7 broadcast_in_dim.10
  30.3 15.3 %scatter_fusion = bf16[64,4,384]{2,1,0:T(4,128)(2,1)} fusion(bf16[64,4,384]{2,1,0:T(4,128)(2,1)} %broadcast_in_dim.10, s32[128]{0:T(128)S(1)} %get-tuple-element.15, bf16[128,384]{1,0:T(8,128)(2,1)S(1)} %copy-done.1), kind=kCustom, calls=%fused_computation.5 | custom fusion | bytes 295936 | tf_op jit(solution)/shard_map/scatter | solution.py:57
  45.6 0.3 all-to-all-done.1
  45.9 17.3 %all-to-all-start = ((bf16[64,4,384]{2,1,0:T(4,128)(2,1)}), bf16[64,4,384]{2,1,0:T(4,128)(2,1)S(1)}, u32[]{:S(2)}, u32[]{:S(2)}) async-start(bf16[64,4,384]{2,1,0:T(4,128)(2,1)} %scatter_fusion), calls=%async_computation | async-start | bytes 393216 | tf_op jit(solution)/shard_map/all_to_all | solution.py:86
  63.2 2.6 %collective-permute-start = (bf16[32,384]{1,0:T(8,128)(2,1)S(1)}, bf16[32,384]{1,0:T(8,128)(2,1)S(1)}, u32[]{:S(2)}, u32[]{:S(2)}) collective-permute-start(bf16[32,384]{1,0:T(8,128)(2,1)S(1)} %get-tuple-element.24), channel_id=1, source_target_pairs={{0,1},{1,2},{2,3},{3,4},{4,5},{5,6},{6,7},{7,0},{8,9},{9,10},{10,1... | collective-permute-start | bytes 73736 | tf_op jit(solution)/shard_map/ppermute | solution.py:18
  65.8 2.7 %collective-permute-start.1 = (bf16[32,384]{1,0:T(8,128)(2,1)S(1)}, bf16[32,384]{1,0:T(8,128)(2,1)S(1)}, u32[]{:S(2)}, u32[]{:S(2)}) collective-permute-start(bf16[32,384]{1,0:T(8,128)(2,1)S(1)} %get-tuple-element.17), channel_id=1, source_target_pairs={{1,0},{2,1},{3,2},{4,3},{5,4},{6,5},{7,6},{0,7},{9,8},{10,9},{11,1... | collective-permute-start | bytes 73736 | tf_op jit(solution)/shard_map/ppermute | solution.py:20
  68.8 18.6 %all-to-all-done = bf16[64,4,384]{2,1,0:T(4,128)(2,1)S(1)} async-done(((bf16[64,4,384]{2,1,0:T(4,128)(2,1)}), bf16[64,4,384]{2,1,0:T(4,128)(2,1)S(1)}, u32[]{:S(2)}, u32[]{:S(2)}) %all-to-all-start) | async-done | bytes 196640 | tf_op jit(solution)/shard_map/all_to_all | solution.py:86
  87.5 0.5 fusion.1
  88.0 0.2 copy.18
  88.2 0.8 reshape.148
  89.0 4.6 %all-to-all-start.2 = ((bf16[64,4,384]{2,1,0:T(4,128)(2,1)}), bf16[64,4,384]{2,1,0:T(4,128)(2,1)S(1)}, u32[]{:S(2)}, u32[]{:S(2)}) async-start(bf16[64,4,384]{2,1,0:T(4,128)(2,1)} %reshape.148), calls=%async_computation.2 | async-start | bytes 393216 | tf_op jit(solution)/shard_map/all_to_all | solution.py:90
  93.7 0.9 gather_fusion.1
  94.6 0.9 gather_fusion.2
  95.5 0.9 gather_fusion.3
  96.3 0.9 gather_fusion.4
  97.2 18.2 %all-to-all-done.2 = bf16[64,4,384]{2,1,0:T(4,128)(2,1)S(1)} async-done(((bf16[64,4,384]{2,1,0:T(4,128)(2,1)}), bf16[64,4,384]{2,1,0:T(4,128)(2,1)S(1)}, u32[]{:S(2)}, u32[]{:S(2)}) %all-to-all-start.2) | async-done | bytes 196640 | tf_op jit(solution)/shard_map/all_to_all | solution.py:90
  115.4 1.2 %gather_fusion = bf16[128,384]{1,0:T(8,128)(2,1)S(1)} fusion(bf16[64,4,384]{2,1,0:T(4,128)(2,1)S(1)} %all-to-all-done.2, s32[128]{0:T(128)S(1)} %bitcast.50), kind=kCustom, calls=%fused_computation | custom fusion | bytes 197632 | tf_op jit(solution)/shard_map/gather | solution.py:91
  116.7 0.7 fusion.11
  (26 shorter events, 0.7 us)
Async XLA Ops:
  0.0 87.5 %copy-start = (bf16[1,4,3,128,128]{4,3,2,1,0:T(8,128)(2,1)S(1)}, bf16[1,4,3,128,128]{4,3,2,1,0:T(8,128)(2,1)}, u32[]{:S(2)}) copy-start(bf16[1,4,3,128,128]{4,3,2,1,0:T(8,128)(2,1)} %param.9) | copy-start | bytes 1179652
  0.0 0.7 copy-start.3
  0.9 0.7 copy-start.4
  8.9 37.0 %all-to-all-start.1 = ((bf16[64,1,4]{2,1,0:T(2,128)(2,1)}), bf16[64,1,4]{2,1,0:T(2,128)(2,1)S(1)}, u32[]{:S(2)}, u32[]{:S(2)}) async-start(bf16[64,1,4]{2,1,0:T(2,128)(2,1)} %copy.16), calls=%async_computation.1 | async-start | bytes 65536 | tf_op jit(solution)/shard_map/all_to_all | solution.py:87
  29.4 0.9 copy-start.1
  45.9 41.5 %all-to-all-start = ((bf16[64,4,384]{2,1,0:T(4,128)(2,1)}), bf16[64,4,384]{2,1,0:T(4,128)(2,1)S(1)}, u32[]{:S(2)}, u32[]{:S(2)}) async-start(bf16[64,4,384]{2,1,0:T(4,128)(2,1)} %scatter_fusion), calls=%async_computation | async-start | bytes 393216 | tf_op jit(solution)/shard_map/all_to_all | solution.py:86
  63.2 30.5 %collective-permute-start = (bf16[32,384]{1,0:T(8,128)(2,1)S(1)}, bf16[32,384]{1,0:T(8,128)(2,1)S(1)}, u32[]{:S(2)}, u32[]{:S(2)}) collective-permute-start(bf16[32,384]{1,0:T(8,128)(2,1)S(1)} %get-tuple-element.24), channel_id=1, source_target_pairs={{0,1},{1,2},{2,3},{3,4},{4,5},{5,6},{6,7},{7,0},{8,9},{9,10},{10,1... | collective-permute-start | bytes 73736 | tf_op jit(solution)/shard_map/ppermute | solution.py:18
  65.8 27.9 %collective-permute-start.1 = (bf16[32,384]{1,0:T(8,128)(2,1)S(1)}, bf16[32,384]{1,0:T(8,128)(2,1)S(1)}, u32[]{:S(2)}, u32[]{:S(2)}) collective-permute-start(bf16[32,384]{1,0:T(8,128)(2,1)S(1)} %get-tuple-element.17), channel_id=1, source_target_pairs={{1,0},{2,1},{3,2},{4,3},{5,4},{6,5},{7,6},{0,7},{9,8},{10,9},{11,1... | collective-permute-start | bytes 73736 | tf_op jit(solution)/shard_map/ppermute | solution.py:20
  89.0 4.6 %copy-start.2 = (s32[4,128]{1,0:T(4,128)S(1)}, s32[4,128]{1,0:T(4,128)}, u32[]{:S(2)}) copy-start(s32[4,128]{1,0:T(4,128)} %param.8) | copy-start | bytes 6148
  89.0 26.4 %all-to-all-start.2 = ((bf16[64,4,384]{2,1,0:T(4,128)(2,1)}), bf16[64,4,384]{2,1,0:T(4,128)(2,1)S(1)}, u32[]{:S(2)}, u32[]{:S(2)}) async-start(bf16[64,4,384]{2,1,0:T(4,128)(2,1)} %reshape.148), calls=%async_computation.2 | async-start | bytes 393216 | tf_op jit(solution)/shard_map/all_to_all | solution.py:90

commit v2 on v1

v2 whole, which is shorter than its diff:
```python
import functools

import jax
import jax.numpy as jnp
from jax import lax
from jax.experimental import pallas as pl
from jax.experimental.pallas import tpu as pltpu
from jax.sharding import PartitionSpec as P

MESH = pl.DeviceIdType.MESH
F32 = jnp.float32
BF16 = jnp.bfloat16
viscosity = 0.25


def kernel(sizes, air, owner, cost, conn, blocks, out, ext, owner_v, cost_v, conn_v, blocks_v, pick, pick_t, wt, send,
           recv, back, home, load_sem, halo_send, halo_recv, send_sem, recv_sem, back_send, back_recv):
    rows, cols, cap, halo, groups = sizes
    row, col = lax.axis_index("row"), lax.axis_index("col")
    left, right = lax.rem(col + cols - 1, cols), lax.rem(col + 1, cols)
    local, feat = air.shape
    classes, fields, levels = blocks_v.shape[:3]
    slots = rows * cap

    barrier = pltpu.get_barrier_semaphore()

    def greet(i, carry):
        pl.semaphore_signal(barrier, inc=1, device_id=(row ^ (rows - 1 - i), col), device_id_type=MESH)
        return carry

    lax.fori_loop(0, rows - 1, greet, 0)
    for side in (left, right):
        pl.semaphore_signal(barrier, inc=1, device_id=(row, side), device_id_type=MESH)

    center = ext.at[pl.ds(halo, local)]
    loads = [
        pltpu.make_async_copy(src, dst, load_sem.at[i])
        for i, (src, dst) in enumerate(
            ((owner, owner_v), (cost, cost_v), (air, center), (conn, conn_v), (blocks, blocks_v))
        )
    ]
    for load in loads:
        load.start()

    loads[0].wait()
    target = jnp.broadcast_to(owner_v[...], (local, local)).astype(F32)
    sub = lax.broadcasted_iota(jnp.int32, (local, local), 0)
    lane = lax.broadcasted_iota(jnp.int32, (local, local), 1)
    same = jnp.where((target == target.T) & (sub < lane), 1.0, 0.0)
    rank = jnp.sum(same, axis=0, keepdims=True).astype(jnp.int32)
    key = (owner_v[...] ^ row) * cap + rank
    slot_id = lax.broadcasted_iota(jnp.int32, (slots, local), 0)
    hit = jnp.where(slot_id == key, 1.0, 0.0)
    loads[1].wait()
    label = jnp.sum(hit * cost_v[...].astype(F32), axis=1, keepdims=True)
    pick[...] = hit.astype(BF16)
    loads[2].wait()
    packed = jnp.dot(pick[...], ext[pl.ds(halo, local), :], preferred_element_type=F32)
    packed = jnp.concatenate([packed, jnp.broadcast_to(label, (slots, levels))], axis=1)
    send[...] = packed.reshape(rows, cap, feat + levels).astype(BF16)

    pl.semaphore_wait(barrier, rows + 1)

    def forward(group):
        low, high = groups[group]

        def one(i, carry):
            j = high - 1 - i
            pltpu.make_async_remote_copy(
                send.at[j], recv.at[j], send_sem, recv_sem.at[group], device_id=(row ^ j, col), device_id_type=MESH
            ).start()
            return carry

        lax.fori_loop(0, high - max(low, 1), one, 0)

    halos = [
        pltpu.make_async_remote_copy(
            ext.at[pl.ds(local, halo)], ext.at[pl.ds(0, halo)], halo_send.at[0], halo_recv.at[0],
            device_id=(row, right), device_id_type=MESH,
        ),
        pltpu.make_async_remote_copy(
            ext.at[pl.ds(halo, halo)], ext.at[pl.ds(halo + local, halo)], halo_send.at[1], halo_recv.at[1],
            device_id=(row, left), device_id_type=MESH,
        ),
    ]
    for group in range(len(groups)):
        forward(group)
        if group == 0:
            for copy in halos:
                copy.start()
    recv[0] = send[0]

    pick_t[...] = pick[...].T
    loads[4].wait()
    for f in range(fields):
        for c in range(classes):
            wt[f, pl.ds(c * levels, levels), :] = blocks_v[c, f].T
    loads[3].wait()

    def laplace():
        for copy in halos:
            copy.wait()
        place = lax.broadcasted_iota(jnp.int32, (local + 2 * halo, local), 0)
        spot = lax.broadcasted_iota(jnp.int32, (1, local), 1) + halo
        count = jnp.where(place == spot, -float(conn_v.shape[0]), 0.0)
        for k in range(conn_v.shape[0]):
            count += jnp.where(place == spot + conn_v[pl.ds(k, 1), :], 1.0, 0.0)
        out[...] = viscosity * jnp.dot(count.T.astype(BF16), ext[...], preferred_element_type=F32)

    def wait_for(buffer, sem, number):
        part = buffer.at[pl.ds(0, number)]
        pltpu.make_async_copy(part, part, sem).wait()

    def work(group):
        low, high = groups[group]
        number = high - low
        wait_for(recv, recv_sem.at[group], high - max(low, 1))
        block = recv[pl.ds(low, number)].astype(F32).reshape(number * cap, feat + levels)
        tag = block[:, feat:]
        made = []
        for f in range(fields):
            part = block[:, f * levels : (f + 1) * levels]
            spread = jnp.concatenate([jnp.where(tag == float(c), part, 0.0).astype(BF16) for c in range(classes)], axis=1)
            made.append(jnp.dot(spread, wt[f], preferred_element_type=F32))
        back[pl.ds(low, number)] = jnp.concatenate(made, axis=1).reshape(number, cap, feat).astype(BF16)

        def one(i, carry):
            j = high - 1 - i
            pltpu.make_async_remote_copy(
                back.at[j], home.at[j], back_send, back_recv, device_id=(row ^ j, col), device_id_type=MESH
            ).start()
            return carry

        lax.fori_loop(0, high - max(low, 1), one, 0)
        if low == 0:
            home[0] = back[0]

    near = len(groups) - 1
    work(near)
    laplace()
    for group in range(near):
        work(group)
    wait_for(home, back_recv, rows - 1)
    returned = home[...].astype(F32).reshape(slots, feat).astype(BF16)
    out[...] += jnp.dot(pick_t[...], returned, preferred_element_type=F32)
    wait_for(send, send_sem, rows - 1)
    wait_for(back, back_send, rows - 1)


def per_device(rows, cols, air, owner, cost, conn, blocks):
    local, feat = air.shape
    classes, fields, levels = blocks.shape[1:4]
    halo = local // 4
    cap = 2 * local // rows
    slots = rows * cap
    step = rows // 8
    groups = tuple((low, low + step) for low in range(rows - step, rows // 2 - 1, -step)) + ((0, rows // 2),)
    n = len(groups)
    sizes = (rows, cols, cap, halo, groups)
    total = pl.pallas_call(
        functools.partial(kernel, sizes),
        out_shape=jax.ShapeDtypeStruct((local, feat), F32),
        in_specs=[pl.BlockSpec(memory_space=pl.ANY)] * 5,
        out_specs=pl.BlockSpec(memory_space=pltpu.VMEM),
        scratch_shapes=[
            pltpu.VMEM((local + 2 * halo, feat), BF16),
            pltpu.VMEM((1, local), jnp.int32),
            pltpu.VMEM((1, local), jnp.int32),
            pltpu.VMEM(conn.shape, jnp.int32),
            pltpu.VMEM((classes, fields, levels, levels), BF16),
            pltpu.VMEM((slots, local), BF16),
            pltpu.VMEM((local, slots), BF16),
            pltpu.VMEM((fields, classes * levels, levels), BF16),
            pltpu.VMEM((rows, cap, feat + levels), BF16),
            pltpu.VMEM((rows, cap, feat + levels), BF16),
            pltpu.VMEM((rows, cap, feat), BF16),
            pltpu.VMEM((rows, cap, feat), BF16),
            pltpu.SemaphoreType.DMA((5,)),
            pltpu.SemaphoreType.DMA((2,)),
            pltpu.SemaphoreType.DMA((2,)),
            pltpu.SemaphoreType.DMA,
            pltpu.SemaphoreType.DMA((n,)),
            pltpu.SemaphoreType.DMA,
            pltpu.SemaphoreType.DMA,
        ],
        compiler_params=pltpu.CompilerParams(collective_id=0, has_side_effects=True),
    )(air, owner.reshape(1, local), cost.reshape(1, local), conn, blocks.reshape(blocks.shape[1:]))
    return total.astype(BF16)


def solution(mesh):
    return jax.shard_map(
        functools.partial(per_device, mesh.shape["row"], mesh.shape["col"]),
        mesh=mesh,
        in_specs=(
            P(("row", "col"), None),
            P(("row", "col"), None),
            P(("row", "col")),
            P(None, ("row", "col")),
            P(("row", "col"), None, None, None, None),
        ),
        out_specs=P(("row", "col"), None),
        check_vma=False,
    )
```

time: 118 us -> 50.9 us (0.43)
  Pallas kernels: 0 us -> 49.1 us
  starting transfers between devices: 47.6 us -> 0 us
  waiting for transfers between devices: 37.1 us -> 0 us
  local copies, waits for them, and re-layouts: 30.9 us -> 0 us
    pallas_call x0 -> x1, Pallas kernels: none -> 49.1 us  [per_device(): pl.pallas_call(functools.partial(kernel, sizes), out_shape=jax.ShapeDtype...]
    all_to_all x3 -> x0, starting transfers between devices: 42.4 us -> none  [the longest x1 20.5 us: per_device(): lax.all_to_all(labels_out, 'row', split_axis=0, concat_axis=0, tiled=True)]
    all_to_all x3 -> x0, waiting for transfers between devices: 37.1 us -> none  [the longest x1 18.6 us: per_device(): lax.all_to_all(outgoing, 'row', split_axis=0, concat_axis=0, tiled=True)]
    scatter x2 -> x0, local copies, waits for them, and re-layouts: 21.9 us -> none  [the longest x1 15.3 us: pack_slots(): outgoing = jnp.zeros((groups, capacity, air_state.shape[1]), jnp.bfloat16...]
    ppermute x2 -> x0, starting transfers between devices: 5.28 us -> none  [the longest x1 2.69 us: padded(): lax.ppermute(head, axis, [((i + 1) % count, i) for i in range(count)])]
    gather x5 -> x0, local copies, waits for them, and re-layouts: 4.69 us -> none  [the longest x4 3.46 us: per_device(): extended[places + connectivity[partner]].astype(jnp.float32) - center]
    unnamed x12 -> x0, local copies, waits for them, and re-layouts: 1.54 us -> none
  transfers between devices with their start and end apart: 5 -> 0, of which waited for: 3 -> 0; matrix products, arithmetic and copies ran while one was open for 18% -> 0% of each run, Pallas kernels for 0% -> 0%
where the time goes in v2:
time: 50.9 us; the launch traced here: 50.7 us
  Pallas kernels  49.1 us (96%)
  other arithmetic  1.58 us (3%)
    pallas_call x1, Pallas kernels, per_device(): pl.pallas_call(functools.partial(kernel, sizes), out_shape=jax.ShapeDtype...  49.1 us
    convert_element_type x1, other arithmetic, per_device(): return total.astype(BF16)  1.58 us

profile of v2, /device:TPU:33, one launch (start us, length us, event | category | flops | bytes accessed | tf_op | source)
XLA Modules:
  0.0 50.7 jit_solution(10796575099699704862)
XLA Ops:
  0.0 49.1 %shard_map.55 = f32[128,384]{1,0:T(8,128)} custom-call(bf16[128,384]{1,0:T(8,128)(2,1)} %air.1, s32[1,128]{1,0:T(1,128)} %bitcast.4, s32[1,128]{1,0:T(1,128)} %bitcast.5, s32[4,128]{1,0:T(4,128)} %conn.1, bf16[4,3,128,128]{3,2,1,0:T(8,128)(2,1)} %bitcast.3), custom_call_target="tpu_custom_call" | custom-call | tf_op jit(solution)/shard_map/pallas_call | solution.py:160
  49.1 1.6 %convert_element_type.3 = bf16[128,384]{1,0:T(8,128)(2,1)} convert(f32[128,384]{1,0:T(8,128)} %shard_map.55) | non-fusion elementwise | flops 49152 | bytes 294912 | tf_op jit(solution)/shard_map/convert_element_type | solution.py:188

commit v3 on v2

--- a/solution.py
+++ b/solution.py
@@ -14,13 +14,15 @@
 
 
 def kernel(sizes, air, owner, cost, conn, blocks, out, ext, owner_v, cost_v, conn_v, blocks_v, pick, pick_t, wt, send,
-           recv, back, home, load_sem, halo_send, halo_recv, send_sem, recv_sem, back_send, back_recv):
+           recv, back, home, tag_out, tag_in, tags, far_tag, load_sem, halo_send, halo_recv, far_send, near_send, recv_sem,
+           tag_send, tag_recv, pass_send, pass_recv, back_send, back_recv):
     rows, cols, cap, halo, groups = sizes
     row, col = lax.axis_index("row"), lax.axis_index("col")
     left, right = lax.rem(col + cols - 1, cols), lax.rem(col + 1, cols)
     local, feat = air.shape
     classes, fields, levels = blocks_v.shape[:3]
-    slots = rows * cap
+    slots, half = rows * cap, rows // 2
+    near = len(groups) - 1
 
     barrier = pltpu.get_barrier_semaphore()
 
@@ -56,22 +58,35 @@
     pick[...] = hit.astype(BF16)
     loads[2].wait()
     packed = jnp.dot(pick[...], ext[pl.ds(halo, local), :], preferred_element_type=F32)
+    classes_row = jnp.broadcast_to(cost_v[...].astype(F32), (8, local)).astype(BF16)
+    tag_row = lax.dot_general(classes_row, pick[pl.ds(half * cap, half * cap), :], (((1,), (1,)), ((), ())), preferred_element_type=F32)
+    tag_out[...] = tag_row[:1]
     packed = jnp.concatenate([packed, jnp.broadcast_to(label, (slots, levels))], axis=1)
     send[...] = packed.reshape(rows, cap, feat + levels).astype(BF16)
 
     pl.semaphore_wait(barrier, rows + 1)
 
+    tag_copy = pltpu.make_async_remote_copy(
+        tag_out, tag_in, tag_send, tag_recv, device_id=(row ^ half, col), device_id_type=MESH
+    )
+
+    def peers(low, high, copy):
+        def one(i, carry):
+            copy(high - 1 - i).start()
+            return carry
+
+        lax.fori_loop(0, high - max(low, 1), one, 0)
+
+    def remote(src, dst, j, send_at, recv_at):
+        return pltpu.make_async_remote_copy(src, dst, send_at, recv_at, device_id=(row ^ j, col), device_id_type=MESH)
+
     def forward(group):
-        low, high = groups[group]
-
-        def one(i, carry):
-            j = high - 1 - i
-            pltpu.make_async_remote_copy(
-                send.at[j], recv.at[j], send_sem, recv_sem.at[group], device_id=(row ^ j, col), device_id_type=MESH
-            ).start()
-            return carry
-
-        lax.fori_loop(0, high - max(low, 1), one, 0)
+        if group == near:
+            peers(*groups[group], lambda j: remote(send.at[j], recv.at[j], j, near_send, recv_sem.at[group]))
+        else:
+            peers(*groups[group], lambda j: remote(
+                send.at[j, :, pl.ds(0, feat)], recv.at[j, :, pl.ds(0, feat)], j, far_send, recv_sem.at[group]
+            ))
 
     halos = [
         pltpu.make_async_remote_copy(
@@ -83,6 +98,7 @@
             device_id=(row, left), device_id_type=MESH,
         ),
     ]
+    tag_copy.start()
     for group in range(len(groups)):
         forward(group)
         if group == 0:
@@ -107,44 +123,49 @@
             count += jnp.where(place == spot + conn_v[pl.ds(k, 1), :], 1.0, 0.0)
         out[...] = viscosity * jnp.dot(count.T.astype(BF16), ext[...], preferred_element_type=F32)
 
-    def wait_for(buffer, sem, number):
-        part = buffer.at[pl.ds(0, number)]
+    def wait_for(part, sem):
         pltpu.make_async_copy(part, part, sem).wait()
 
     def work(group):
         low, high = groups[group]
         number = high - low
-        wait_for(recv, recv_sem.at[group], high - max(low, 1))
-        block = recv[pl.ds(low, number)].astype(F32).reshape(number * cap, feat + levels)
-        tag = block[:, feat:]
+        if group == near:
+            wait_for(recv.at[pl.ds(1, number - 1)], recv_sem.at[group])
+            tag = recv[pl.ds(low, number), :, feat:].astype(F32).reshape(number * cap, levels)
+        else:
+            wait_for(recv.at[pl.ds(low, number), :, pl.ds(0, feat)], recv_sem.at[group])
+            tag = far_tag[pl.ds((low - half) * cap, number * cap), :]
+        block = recv[pl.ds(low, number), :, :feat].astype(F32).reshape(number * cap, feat)
         made = []
         for f in range(fields):
             part = block[:, f * levels : (f + 1) * levels]
             spread = jnp.concatenate([jnp.where(tag == float(c), part, 0.0).astype(BF16) for c in range(classes)], axis=1)
             made.append(jnp.dot(spread, wt[f], preferred_element_type=F32))
         back[pl.ds(low, number)] = jnp.concatenate(made, axis=1).reshape(number, cap, feat).astype(BF16)
-
-        def one(i, carry):
-            j = high - 1 - i
-            pltpu.make_async_remote_copy(
-                back.at[j], home.at[j], back_send, back_recv, device_id=(row ^ j, col), device_id_type=MESH
-            ).start()
-            return carry
-
-        lax.fori_loop(0, high - max(low, 1), one, 0)
-        if low == 0:
-            home[0] = back[0]
-
-    near = len(groups) - 1
+        peers(low, high, lambda j: remote(back.at[j], home.at[j], j, back_send, back_recv))
+
+    tag_copy.wait()
+    peers(1, half, lambda j: remote(tag_in, tags.at[j], j, pass_send, pass_recv))
+    tags[0] = tag_in[...]
+
     work(near)
+    home[0] = back[0]
     laplace()
+
+    wait_for(tags.at[pl.ds(1, half - 1)], pass_recv)
+    rows_of = jnp.broadcast_to(tags[...], (half, cap, half * cap)).reshape(half * cap, half * cap)
+    mine = lax.broadcasted_iota(jnp.int32, rows_of.shape, 0) == lax.broadcasted_iota(jnp.int32, rows_of.shape, 1)
+    far_tag[...] = jnp.broadcast_to(jnp.sum(jnp.where(mine, rows_of, 0.0), axis=1, keepdims=True), (half * cap, levels))
+
     for group in range(near):
         work(group)
-    wait_for(home, back_recv, rows - 1)
+    wait_for(home.at[pl.ds(1, rows - 1)], back_recv)
     returned = home[...].astype(F32).reshape(slots, feat).astype(BF16)
     out[...] += jnp.dot(pick_t[...], returned, preferred_element_type=F32)
-    wait_for(send, send_sem, rows - 1)
-    wait_for(back, back_send, rows - 1)
+    wait_for(send.at[pl.ds(half, half), :, pl.ds(0, feat)], far_send)
+    wait_for(send.at[pl.ds(1, half - 1)], near_send)
+    wait_for(tags.at[pl.ds(1, half - 1)], pass_send)
+    wait_for(back.at[pl.ds(1, rows - 1)], back_send)
 
 
 def per_device(rows, cols, air, owner, cost, conn, blocks):
@@ -159,7 +180,7 @@
     sizes = (rows, cols, cap, halo, groups)
     total = pl.pallas_call(
         functools.partial(kernel, sizes),
-        out_shape=jax.ShapeDtypeStruct((local, feat), F32),
+        out_shape=pltpu.VMEM((local, feat), F32),
         in_specs=[pl.BlockSpec(memory_space=pl.ANY)] * 5,
         out_specs=pl.BlockSpec(memory_space=pltpu.VMEM),
         scratch_shapes=[
@@ -175,11 +196,20 @@
             pltpu.VMEM((rows, cap, feat + levels), BF16),
             pltpu.VMEM((rows, cap, feat), BF16),
             pltpu.VMEM((rows, cap, feat), BF16),
+            pltpu.VMEM((1, slots // 2), F32),
+            pltpu.VMEM((1, slots // 2), F32),
+            pltpu.VMEM((rows // 2, 1, slots // 2), F32),
+            pltpu.VMEM((slots // 2, levels), F32),
             pltpu.SemaphoreType.DMA((5,)),
             pltpu.SemaphoreType.DMA((2,)),
             pltpu.SemaphoreType.DMA((2,)),
             pltpu.SemaphoreType.DMA,
+            pltpu.SemaphoreType.DMA,
             pltpu.SemaphoreType.DMA((n,)),
+            pltpu.SemaphoreType.DMA,
+            pltpu.SemaphoreType.DMA,
+            pltpu.SemaphoreType.DMA,
+            pltpu.SemaphoreType.DMA,
             pltpu.SemaphoreType.DMA,
             pltpu.SemaphoreType.DMA,
         ],

time: 50.9 us -> 46.2 us (0.908)
  Pallas kernels: 49.1 us -> 45.4 us
  other arithmetic: 1.58 us -> 0.65 us
    pallas_call x1, Pallas kernels: 49.1 us -> 45.4 us  [per_device(): pl.pallas_call(functools.partial(kernel, sizes), out_shape=pltpu.VMEM((lo...]
    convert_element_type x1, other arithmetic: 1.58 us -> 0.65 us  [per_device(): return total.astype(BF16)]
where the time goes in v3:
time: 46.2 us; the launch traced here: 46.1 us
  Pallas kernels  45.4 us (98%)
  other arithmetic  0.65 us (1%)
    pallas_call x1, Pallas kernels, per_device(): pl.pallas_call(functools.partial(kernel, sizes), out_shape=pltpu.VMEM((lo...  45.4 us

profile of v3, /device:TPU:33, one launch (start us, length us, event | category | flops | bytes accessed | tf_op | source)
XLA Modules:
  0.0 46.1 jit_solution(7601852534890511069)
XLA Ops:
  0.0 45.4 %shard_map.55 = f32[128,384]{1,0:T(8,128)S(1)} custom-call(bf16[128,384]{1,0:T(8,128)(2,1)} %air.1, s32[1,128]{1,0:T(1,128)} %bitcast.4, s32[1,128]{1,0:T(1,128)} %bitcast.5, s32[4,128]{1,0:T(4,128)} %conn.1, bf16[4,3,128,128]{3,2,1,0:T(8,128)(2,1)} %bitcast.3), custom_call_target="tpu_custom_call" | custom-call | tf_op jit(solution)/shard_map/pallas_call | solution.py:181
  45.4 0.7 %convert_element_type.3 = bf16[128,384]{1,0:T(8,128)(2,1)} convert(f32[128,384]{1,0:T(8,128)S(1)} %shard_map.55) | non-fusion elementwise | flops 49152 | bytes 294912 | tf_op jit(solution)/shard_map/convert_element_type | solution.py:218

commit v4 on v3

--- a/solution.py
+++ b/solution.py
@@ -98,20 +98,38 @@
             device_id=(row, left), device_id_type=MESH,
         ),
     ]
+    def wait_for(part, sem):
+        pltpu.make_async_copy(part, part, sem).wait()
+
+    def turn():
+        pick_t[...] = pick[...].T
+        loads[4].wait()
+        for f in range(fields):
+            for c in range(classes):
+                wt[f, pl.ds(c * levels, levels), :] = blocks_v[c, f].T
+        loads[3].wait()
+
+
+    first = col < 2
+    held = (row >= half) & (col >= 2)
     tag_copy.start()
-    for group in range(len(groups)):
-        forward(group)
-        if group == 0:
-            for copy in halos:
-                copy.start()
+    for copy in halos:
+        copy.start()
+
+    @pl.when(first)
+    def _():
+        for group in range(near):
+            forward(group)
+
+    forward(near)
+
+    @pl.when(jnp.logical_not(first))
+    def _():
+        for group in range(near):
+            forward(group)
+
+    turn()
     recv[0] = send[0]
-
-    pick_t[...] = pick[...].T
-    loads[4].wait()
-    for f in range(fields):
-        for c in range(classes):
-            wt[f, pl.ds(c * levels, levels), :] = blocks_v[c, f].T
-    loads[3].wait()
 
     def laplace():
         for copy in halos:
@@ -123,8 +141,9 @@
             count += jnp.where(place == spot + conn_v[pl.ds(k, 1), :], 1.0, 0.0)
         out[...] = viscosity * jnp.dot(count.T.astype(BF16), ext[...], preferred_element_type=F32)
 
-    def wait_for(part, sem):
-        pltpu.make_async_copy(part, part, sem).wait()
+    def arrived(group):
+        low, high = groups[group]
+        wait_for(recv.at[pl.ds(low, high - low), :, pl.ds(0, feat)], recv_sem.at[group])
 
     def work(group):
         low, high = groups[group]
@@ -133,7 +152,10 @@
             wait_for(recv.at[pl.ds(1, number - 1)], recv_sem.at[group])
             tag = recv[pl.ds(low, number), :, feat:].astype(F32).reshape(number * cap, levels)
         else:
-            wait_for(recv.at[pl.ds(low, number), :, pl.ds(0, feat)], recv_sem.at[group])
+            @pl.when(jnp.logical_not(held))
+            def _():
+                arrived(group)
+
             tag = far_tag[pl.ds((low - half) * cap, number * cap), :]
         block = recv[pl.ds(low, number), :, :feat].astype(F32).reshape(number * cap, feat)
         made = []
@@ -156,6 +178,11 @@
     rows_of = jnp.broadcast_to(tags[...], (half, cap, half * cap)).reshape(half * cap, half * cap)
     mine = lax.broadcasted_iota(jnp.int32, rows_of.shape, 0) == lax.broadcasted_iota(jnp.int32, rows_of.shape, 1)
     far_tag[...] = jnp.broadcast_to(jnp.sum(jnp.where(mine, rows_of, 0.0), axis=1, keepdims=True), (half * cap, levels))
+
+    @pl.when(held)
+    def _():
+        for group in range(near):
+            arrived(group)
 
     for group in range(near):
         work(group)

time: 46.2 us -> 45.3 us (0.981)
  Pallas kernels: 45.4 us -> 44.3 us
    pallas_call x1, Pallas kernels: 45.4 us -> 44.3 us  [per_device(): pl.pallas_call(functools.partial(kernel, sizes), out_shape=pltpu.VMEM((lo...]
where the time goes in v4:
time: 45.3 us; the launch traced here: 45 us
  Pallas kernels  44.3 us (98%)
  other arithmetic  0.65 us (1%)
    pallas_call x1, Pallas kernels, per_device(): pl.pallas_call(functools.partial(kernel, sizes), out_shape=pltpu.VMEM((lo...  44.3 us

profile of v4, /device:TPU:33, one launch (start us, length us, event | category | flops | bytes accessed | tf_op | source)
XLA Modules:
  0.0 45.0 jit_solution(18204745391108328017)
XLA Ops:
  0.0 44.3 %shard_map.55 = f32[128,384]{1,0:T(8,128)S(1)} custom-call(bf16[128,384]{1,0:T(8,128)(2,1)} %air.1, s32[1,128]{1,0:T(1,128)} %bitcast.4, s32[1,128]{1,0:T(1,128)} %bitcast.5, s32[4,128]{1,0:T(4,128)} %conn.1, bf16[4,3,128,128]{3,2,1,0:T(8,128)(2,1)} %bitcast.3), custom_call_target="tpu_custom_call" | custom-call | tf_op jit(solution)/shard_map/pallas_call | solution.py:208
  44.3 0.7 %convert_element_type.3 = bf16[128,384]{1,0:T(8,128)(2,1)} convert(f32[128,384]{1,0:T(8,128)S(1)} %shard_map.55) | non-fusion elementwise | flops 49152 | bytes 294912 | tf_op jit(solution)/shard_map/convert_element_type | solution.py:245

commit v5 on v4

--- a/solution.py
+++ b/solution.py
@@ -110,7 +110,7 @@
         loads[3].wait()
 
 
-    first = col < 2
+    first = (col < 2) | (row >= half)
     held = (row >= half) & (col >= 2)
     tag_copy.start()
     for copy in halos:
@@ -125,10 +125,14 @@
 
     @pl.when(jnp.logical_not(first))
     def _():
+        turn()
         for group in range(near):
             forward(group)
 
-    turn()
+    @pl.when(first)
+    def _():
+        turn()
+
     recv[0] = send[0]
 
     def laplace():

time: 45.3 us -> 45.3 us (level)
  the two profiles are of different devices: /device:TPU:33 before, /device:TPU:1 now
where the time goes in v5:
time: 45.3 us; the launch traced here: 45.2 us
  Pallas kernels  44.5 us (98%)
  other arithmetic  0.65 us (1%)
    pallas_call x1, Pallas kernels, per_device(): pl.pallas_call(functools.partial(kernel, sizes), out_shape=pltpu.VMEM((lo...  44.5 us

profile of v5, /device:TPU:1, one launch (start us, length us, event | category | flops | bytes accessed | tf_op | source)
XLA Modules:
  0.0 45.2 jit_solution(5876347032016016967)
XLA Ops:
  0.0 44.5 %shard_map.55 = f32[128,384]{1,0:T(8,128)S(1)} custom-call(bf16[128,384]{1,0:T(8,128)(2,1)} %air.1, s32[1,128]{1,0:T(1,128)} %bitcast.4, s32[1,128]{1,0:T(1,128)} %bitcast.5, s32[4,128]{1,0:T(4,128)} %conn.1, bf16[4,3,128,128]{3,2,1,0:T(8,128)(2,1)} %bitcast.3), custom_call_target="tpu_custom_call" | custom-call | tf_op jit(solution)/shard_map/pallas_call | solution.py:212
  44.5 0.7 %convert_element_type.3 = bf16[128,384]{1,0:T(8,128)(2,1)} convert(f32[128,384]{1,0:T(8,128)S(1)} %shard_map.55) | non-fusion elementwise | flops 49152 | bytes 294912 | tf_op jit(solution)/shard_map/convert_element_type | solution.py:249

commit v6 on v5

--- a/solution.py
+++ b/solution.py
@@ -205,7 +205,7 @@
     halo = local // 4
     cap = 2 * local // rows
     slots = rows * cap
-    step = rows // 8
+    step = rows // 16
     groups = tuple((low, low + step) for low in range(rows - step, rows // 2 - 1, -step)) + ((0, rows // 2),)
     n = len(groups)
     sizes = (rows, cols, cap, halo, groups)

time: 45.3 us -> 45.3 us (level)
  the two profiles are of different devices: /device:TPU:1 before, /device:TPU:33 now
where the time goes in v6:
time: 45.3 us; the launch traced here: 45.1 us
  Pallas kernels  44.5 us (98%)
  other arithmetic  0.65 us (1%)
    pallas_call x1, Pallas kernels, per_device(): pl.pallas_call(functools.partial(kernel, sizes), out_shape=pltpu.VMEM((lo...  44.5 us

profile of v6, /device:TPU:33, one launch (start us, length us, event | category | flops | bytes accessed | tf_op | source)
XLA Modules:
  0.0 45.1 jit_solution(610346140528377165)
XLA Ops:
  0.0 44.5 %shard_map.55 = f32[128,384]{1,0:T(8,128)S(1)} custom-call(bf16[128,384]{1,0:T(8,128)(2,1)} %air.1, s32[1,128]{1,0:T(1,128)} %bitcast.4, s32[1,128]{1,0:T(1,128)} %bitcast.5, s32[4,128]{1,0:T(4,128)} %conn.1, bf16[4,3,128,128]{3,2,1,0:T(8,128)(2,1)} %bitcast.3), custom_call_target="tpu_custom_call" | custom-call | tf_op jit(solution)/shard_map/pallas_call | solution.py:212
  44.5 0.7 %convert_element_type.3 = bf16[128,384]{1,0:T(8,128)(2,1)} convert(f32[128,384]{1,0:T(8,128)S(1)} %shard_map.55) | non-fusion elementwise | flops 49152 | bytes 294912 | tf_op jit(solution)/shard_map/convert_element_type | solution.py:249
